TPU v7x, 256 devices: a whole 4x4x8 slice. The times are simulated.
256 devices in a mesh: gx: 8 (over z), gy: 8 (over x, core), gz: 4 (over y).
Axes of the slice: x: 4, y: 4, z: 8, core: 2. Of those that a mesh axis runs over, the one named last changes fastest.
Arguments:
- right_side: float32 [5, 64, 16, 2048], P(None, 'gx', 'gz', 'gy'), may hold values from -6 to 6
- conductance: float32 [64, 16, 2048], P('gx', 'gz', 'gy'), may hold values from 0.5 to 1
- blocks: float32 [27, 5, 5], replicated, may hold values from -0.3125 to 0.3125
Outputs:
- solution: float32 [5, 64, 16, 2048], P(None, 'gx', 'gz', 'gy')
- residual: float32 [5, 64, 16, 2048], P(None, 'gx', 'gz', 'gy')
All inputs are finite; a program needn't handle non-finite values.
Results may differ from a plain program's by a relative error of at most 0.00045.
Values sent between devices are 32-bit elements; how exact they have to be, the bound alone decides.
No kernel may reach another device: no remote copies, remote signals or barrier semaphores. Data moves between devices by JAX's collectives and lax.ppermute only.
A program may use at most 192 MiB of HBM per device.

v0:
```python
import functools

import jax
import jax.numpy as jnp
from jax import lax
from jax.experimental import pallas as pl
from jax.experimental.pallas import tpu as pltpu
from jax.sharding import PartitionSpec as P

STEPS = 4
POWERS = 2 * STEPS
VARS = 5
FIELDS = VARS + 1
HALO = POWERS
LANES = 128
CHUNK = 10
PAIRS = [(i, j) for i in range(POWERS + 1) for j in range(i, POWERS + 1)]

F32 = jnp.float32
BF16 = jnp.bfloat16
VMEM = 24 * 1024 * 1024


def lane_iota(rows, lanes=LANES):
    return lax.broadcasted_iota(jnp.int32, (rows, lanes), 1)


def row_iota(rows, lanes=LANES):
    return lax.broadcasted_iota(jnp.int32, (rows, lanes), 0)


def roll_lanes(value, shift):
    shift = shift % LANES
    return value if shift == 0 else pltpu.roll(value, shift, value.ndim - 1)


def pieces_of(value, count):
    pieces = []
    for at in range(count):
        piece = value.astype(BF16)
        pieces.append(piece)
        if at < count - 1:
            value = value - piece.astype(F32)
    return pieces


def pack_kernel(peers, fields_ref, out_ref, first_ref, last_ref, own):
    _, extent_x, extent_z, extent_y = fields_ref.shape
    group = FIELDS * extent_z
    for x_at in range(extent_x):
        for field in range(FIELDS):
            base = x_at * group + field * extent_z
            own[base : base + extent_z, :] = fields_ref[field, x_at]
    rest = extent_x * group - LANES
    own[LANES + rest :, :] = jnp.zeros((LANES - rest, extent_y), F32)
    gap = jnp.zeros((HALO, LANES), F32)
    width = extent_y // peers
    wide = width + 2 * HALO
    halves = lane_iota(wide // 2) < LANES // 2
    for part in range(2):
        turned = []
        for tile in range(extent_y // LANES):
            turned.append(own[part * LANES : (part + 1) * LANES, tile * LANES : (tile + 1) * LANES].T)
        whole = jnp.concatenate([gap] + turned + [gap], axis=0)
        for peer in range(peers):
            strip = whole[peer * width : peer * width + wide]
            if part == 0:
                out_ref[peer, :wide] = strip
            else:
                beside = roll_lanes(strip[wide // 2 :], LANES // 2)
                out_ref[peer, wide:] = jnp.where(halves, strip[: wide // 2], beside)
        for ref, start in ((first_ref, HALO), (last_ref, extent_y)):
            value = whole[start : start + HALO]
            if part == 1:
                value = jnp.where(halves[:HALO], value, roll_lanes(value, LANES // 2))
            ref[part] = value


def edge_kernel(wide, strips_ref, left_ref, right_ref, out_ref):
    peers, rows, _ = strips_ref.shape
    lower = lane_iota(HALO) < LANES // 2
    out_ref[...] = strips_ref[...]
    out_ref[0, :HALO] = left_ref[0]
    out_ref[0, wide : wide + HALO] = jnp.where(lower, left_ref[1], strips_ref[0, wide : wide + HALO])
    out_ref[peers - 1, wide - HALO : wide] = right_ref[0]
    out_ref[peers - 1, rows - HALO :] = jnp.where(lower, strips_ref[peers - 1, rows - HALO :], right_ref[1])


def matrix_kernel(peers, extent_z, rows_ref, spread, matrix):
    size_z = peers * extent_z
    used = VARS * size_z
    group = FIELDS * extent_z

    row, lane = row_iota(LANES, 2 * LANES), lane_iota(LANES, 2 * LANES)
    column = lane % LANES
    wanted = jnp.where(lane < LANES, column // size_z, VARS)
    source_z = (row // group) * extent_z + row % extent_z
    hit = ((row % group) // extent_z == wanted) & (source_z == column % size_z)
    hit = hit & (column < used) & (row < peers * group)
    pick = jnp.where(hit, 1.0, 0.0).astype(BF16)
    for at in range(3):
        spread[at * LANES : (at + 1) * LANES, :] = pick

    row_z = row_iota(size_z)
    lane_z = lane_iota(size_z)
    ahead = jnp.where(lane_z < used, row_z - lane_z % size_z, LANES)
    lanes = lane_iota(used)
    rest = used - (LANES - used)
    blocks = []
    for along_x in range(3):
        parts_y = []
        for along_y in range(3):
            groups = []
            for source in range(VARS):
                total = jnp.zeros((size_z, LANES), F32)
                for along_z in range(3):
                    line = (9 * along_x + 3 * along_z + along_y) * VARS + source
                    total = jnp.where(ahead == along_z - 1, rows_ref[line : line + 1, :], total)
                groups.append(total)
            parts_y.append(jnp.concatenate(groups, axis=0))
        first = jnp.where(lanes < used, parts_y[1], roll_lanes(parts_y[2], used))
        second = jnp.where(lanes < used, parts_y[0], roll_lanes(parts_y[2], 2 * used))
        second = jnp.where(lanes < used + used - (LANES - used), second, 0.0)
        blocks.append(jnp.concatenate([first, second], axis=1))
    blocks.append(jnp.zeros((2 * LANES - 3 * used, 2 * LANES), F32))
    high, low = pieces_of(jnp.concatenate(blocks, axis=0), 2)
    matrix[: 2 * LANES, :] = high
    matrix[2 * LANES : 4 * LANES, :] = high
    matrix[4 * LANES :, :] = low


def powers_kernel(
    own_x, extent_z, before_ref, here_ref, after_ref, spread, matrix, basis_ref, gram_ref, even, odd, cond
):
    peers = here_ref.shape[0]
    wide_y = cond.shape[1]
    size_z = peers * extent_z
    used = VARS * size_z
    group = FIELDS * extent_z
    half = own_x // 2
    wide_x = 3 * own_x
    own_y = wide_y - 2 * HALO

    at_x, at_y, at_z = (lax.axis_index(axis) for axis in ("gx", "gy", "gz"))
    count_x, count_y = lax.axis_size("gx"), lax.axis_size("gy")
    column_y = row_iota(wide_y) + ((at_y * peers + at_z) * own_y - HALO)
    inside_y = (column_y >= 0) & (column_y < count_y * peers * own_y)
    lane = lane_iota(wide_y)
    for block, ref in enumerate((before_ref, here_ref, after_ref)):
        block_x = at_x + (block - 1)
        inside = inside_y & (block_x >= 0) & (block_x < count_x)
        whole, rest = [], []
        for peer in range(peers):
            whole.append(ref[peer, :wide_y])
            packed = ref[peer, wide_y:]
            rest.append(jnp.concatenate([packed, roll_lanes(packed, LANES // 2)], axis=0))

        def moved(peer, start):
            place = peer * group
            if start >= LANES:
                return roll_lanes(rest[peer], place - (start - LANES))
            value = roll_lanes(whole[peer], place - start)
            if start + group > LANES:
                edge = place + LANES - start
                value = jnp.where(lane < edge, value, roll_lanes(rest[peer], edge))
            return value

        for part in range(2):
            gathered = []
            for x_local in range(half):
                start = (part * half + x_local) * group
                total = moved(0, start)
                for peer in range(1, peers):
                    total = jnp.where(lane < peer * group, total, moved(peer, start))
                gathered.append(total)
            split = pieces_of(jnp.concatenate(gathered, axis=0), 3)
            result = jnp.dot(jnp.concatenate(split, axis=1), spread[...], preferred_element_type=F32)
            for x_local in range(half):
                x_at = (block * 2 + part) * half + x_local
                rows = slice(x_local * wide_y, (x_local + 1) * wide_y)
                field = result[rows, :LANES]
                weight = jnp.where(inside, result[rows, LANES:], 0.0)
                cond[x_at] = weight
                even[x_at + 1] = weight * field
                if block == 1:
                    basis_ref[0, part * half + x_local] = field[HALO : HALO + own_y]

    def apply(power, now, later, x_from, count):
        near = [now[x_from + at] for at in range(count + 2)]
        firsts, seconds = [], []
        for at in range(count):
            middle = roll_lanes(near[at + 1], used)
            firsts.append(jnp.where(lane < used, near[at], middle))
            last = roll_lanes(near[at + 2], 2 * used)
            seconds.append(jnp.where(lane < 2 * used - LANES, middle, last))
        stacked = jnp.concatenate(
            [jnp.concatenate(firsts, axis=0), jnp.concatenate(seconds, axis=0)], axis=1
        )
        high, low = pieces_of(stacked, 2)
        product = jnp.dot(jnp.concatenate([high, low, high], axis=1), matrix[...], preferred_element_type=F32)
        for at in range(count):
            x_at = x_from + at
            left = product[at * wide_y : (at + 1) * wide_y, :LANES]
            right = product[at * wide_y : (at + 1) * wide_y, LANES:]
            ahead = jnp.where(lane < LANES - used, roll_lanes(left, -used), roll_lanes(right, -2 * used))
            total = left + pltpu.roll(right, 1, 0) + pltpu.roll(ahead, wide_y - 1, 0)
            weight = cond[x_at]
            value = weight * total
            if 0 <= x_at - own_x < own_x:
                basis_ref[power, x_at - own_x] = value[HALO : HALO + own_y]
            if power < POWERS:
                later[x_at + 1] = weight * value

    slots = (even, odd)
    for power in range(1, POWERS + 1):
        for x_from, x_to in spans(power, wide_x - power):
            apply(power, slots[(power + 1) % 2], slots[power % 2], x_from, x_to - x_from)

    def add(x_at, sums):
        for tile in range(own_y // 8):
            tiles = [basis_ref[power, x_at, tile * 8 : (tile + 1) * 8, :] for power in range(POWERS + 1)]
            sums = tuple(total + tiles[i] * tiles[j] for total, (i, j) in zip(sums, PAIRS))
        return sums

    sums = lax.fori_loop(0, own_x, add, tuple(jnp.zeros((8, LANES), F32) for _ in PAIRS))
    lines = [jnp.sum(total, axis=0, keepdims=True) for total in sums]
    lines.append(jnp.zeros((LANES - len(PAIRS), LANES), F32))
    table = jnp.concatenate(lines, axis=0)
    line = lax.dot_general(
        jnp.ones((8, LANES), F32),
        table,
        (((1,), (1,)), ((), ())),
        precision=lax.Precision.HIGHEST,
        preferred_element_type=F32,
    )[:1]
    gram_ref[...] = line


def spans(start, stop):
    count = -(-(stop - start) // CHUNK)
    marks = [start + (stop - start) * at // count for at in range(count + 1)]
    return list(zip(marks[:-1], marks[1:]))


def solve(gram):
    paired = [[gram[i][j] + gram[i + 1][j] for j in range(STEPS + 1)] for i in range(STEPS)]
    normal = [[paired[i][j] + paired[i][j + 1] for j in range(STEPS)] for i in range(STEPS)]
    target = [paired[i][0] for i in range(STEPS)]
    lower = [[None] * STEPS for _ in range(STEPS)]
    inverse = []
    for col in range(STEPS):
        value = normal[col][col]
        for k in range(col):
            value = value - lower[col][k] * lower[col][k]
        root = jnp.sqrt(value)
        lower[col][col] = root
        inverse.append(1.0 / root)
        for row in range(col + 1, STEPS):
            value = normal[row][col]
            for k in range(col):
                value = value - lower[row][k] * lower[col][k]
            lower[row][col] = value * inverse[col]
    forward = []
    for row in range(STEPS):
        value = target[row]
        for col in range(row):
            value = value - lower[row][col] * forward[col]
        forward.append(value * inverse[row])
    coefs = [None] * STEPS
    for row in range(STEPS - 1, -1, -1):
        value = forward[row]
        for col in range(row + 1, STEPS):
            value = value - lower[col][row] * coefs[col]
        coefs[row] = value * inverse[row]
    return coefs


def remainder(coefs):
    inner = [-(coefs[k - 1] + coefs[k]) for k in range(1, STEPS)]
    return [1.0 - coefs[0]] + inner + [-coefs[STEPS - 1]]


def turn_kernel(peers, basis_ref, out_ref, turned):
    _, own_x, _, _ = basis_ref.shape
    extent_z = out_ref.shape[2] // (own_x * VARS)
    for pair in range(POWERS // 2):
        for x_at in range(own_x):
            both = jnp.concatenate([basis_ref[2 * pair + 1, x_at], basis_ref[2 * pair + 2, x_at]], axis=0)
            turned[pair, x_at] = both.T
            for peer in range(peers):
                for var in range(VARS):
                    source = (var * peers + peer) * extent_z
                    place = (x_at * VARS + var) * extent_z
                    out_ref[peer, pair, place : place + extent_z, :] = turned[
                        pair, x_at, source : source + extent_z, :
                    ]


def finish_kernel(grams_ref, first_ref, *refs):
    parts, (solution_ref, residual_ref, solutions, residuals) = refs[:-4], refs[-4:]
    peers = len(parts)
    _, extent_x, extent_z, extent_y = first_ref.shape
    line = jnp.sum(grams_ref[...], axis=0)
    where = lane_iota(1)
    entry = {}
    for at, (i, j) in enumerate(PAIRS):
        value = jnp.sum(jnp.where(where == at, line, 0.0), axis=1, keepdims=True)
        entry[i, j] = entry[j, i] = value
    first = solve([[entry[i, j] for j in range(STEPS + 1)] for i in range(STEPS + 1)])
    left = remainder(first)
    half = {}
    for i in range(STEPS + 1):
        for j in range(POWERS + 1):
            value = left[0] * entry[i, j]
            for k in range(1, STEPS + 1):
                value = value + left[k] * entry[i + k, j]
            half[i, j] = value
    second_gram = []
    for i in range(STEPS + 1):
        line = []
        for j in range(STEPS + 1):
            value = left[0] * half[i, j]
            for k in range(1, STEPS + 1):
                value = value + left[k] * half[i, j + k]
            line.append(value)
        second_gram.append(line)
    second = solve(second_gram)
    last = remainder(second)
    of_solution = list(first) + [0.0] * STEPS
    of_residual = [0.0] * (POWERS + 1)
    for i in range(STEPS):
        for k in range(STEPS + 1):
            of_solution[i + k] = of_solution[i + k] + second[i] * left[k]
    for i in range(STEPS + 1):
        for k in range(STEPS + 1):
            of_residual[i + k] = of_residual[i + k] + last[i] * left[k]
    of_solution.append(0.0)
    middle = LANES // 2
    pick = lane_iota(1) < middle

    def paired(coefs, pair):
        return jnp.where(pick, coefs[2 * pair + 1], coefs[2 * pair + 2])

    at_z = lax.axis_index("gz")
    for shift, ref in enumerate(parts):
        chunk = lax.rem(at_z + peers - shift, peers)
        for coefs, sums in ((of_solution, solutions), (of_residual, residuals)):
            total = paired(coefs, 0) * ref[0]
            for pair in range(1, POWERS // 2):
                total = total + paired(coefs, pair) * ref[pair]
            sums[chunk] = total + roll_lanes(total, middle)
    lanes = lane_iota(extent_z)
    for x_at in range(extent_x):
        for var in range(VARS):
            place = (x_at * VARS + var) * extent_z
            rows = slice(place, place + extent_z)
            for tile in range(extent_y // LANES):
                columns = slice(tile * LANES, (tile + 1) * LANES)
                first_part = first_ref[var, x_at, :, columns]
                for coefs, sums, ref in (
                    (of_solution, solutions, solution_ref),
                    (of_residual, residuals, residual_ref),
                ):
                    rest = jnp.where(lanes < middle, sums[2 * tile, rows, :], sums[2 * tile + 1, rows, :])
                    ref[var, x_at, :, columns] = coefs[0] * first_part + rest


def call(kernel, out_shape, scratch=(), **more):
    return pl.pallas_call(
        kernel,
        out_shape=out_shape,
        scratch_shapes=scratch,
        compiler_params=pltpu.CompilerParams(vmem_limit_bytes=VMEM),
        **more,
    )


def ring(count):
    up = [(i, (i + 1) % count) for i in range(count)]
    return up, [(j, i) for i, j in up]


def per_device(right_side, conductance, blocks):
    count_x, count_y, count_z = (lax.axis_size(axis) for axis in ("gx", "gy", "gz"))
    _, extent_x, extent_z, extent_y = right_side.shape
    size_z = extent_z * count_z
    own_y = extent_y // count_z
    wide_y = own_y + 2 * HALO

    edge = jax.ShapeDtypeStruct((2, HALO, LANES), F32)
    strips, first, last = call(
        functools.partial(pack_kernel, count_z),
        (jax.ShapeDtypeStruct((count_z, wide_y + wide_y // 2, LANES), F32), edge, edge),
        (pltpu.VMEM((2 * LANES, extent_y), F32),),
    )(jnp.concatenate([right_side, conductance[None]], axis=0))
    up, down = ring(count_y)
    left = lax.ppermute(last, "gy", up)
    right = lax.ppermute(first, "gy", down)
    strips = call(
        functools.partial(edge_kernel, wide_y), jax.ShapeDtypeStruct(strips.shape, F32)
    )(strips, left, right)
    here = lax.all_to_all(strips, "gz", 0, 0, tiled=True)
    up, down = ring(count_x)
    before = lax.ppermute(here, "gx", up)
    after = lax.ppermute(here, "gx", down)

    rows = jnp.repeat(blocks.transpose(0, 2, 1).reshape(-1, VARS), size_z, axis=1)
    rows = jnp.pad(rows, ((0, 1), (0, LANES - VARS * size_z)))
    spread, matrix = call(
        functools.partial(matrix_kernel, count_z, extent_z),
        (
            jax.ShapeDtypeStruct((3 * LANES, 2 * LANES), BF16),
            jax.ShapeDtypeStruct((6 * LANES, 2 * LANES), BF16),
        ),
    )(rows)
    basis, gram = call(
        functools.partial(powers_kernel, extent_x, extent_z),
        (
            jax.ShapeDtypeStruct((POWERS + 1, extent_x, own_y, LANES), F32),
            jax.ShapeDtypeStruct((1, LANES), F32),
        ),
        (
            pltpu.VMEM((3 * extent_x + 2, wide_y, LANES), F32),
            pltpu.VMEM((3 * extent_x + 2, wide_y, LANES), F32),
            pltpu.VMEM((3 * extent_x, wide_y, LANES), F32),
        ),
    )(before, here, after, spread, matrix)

    pairs = [(i, i ^ 1) for i in range(count_y)]
    gram = gram + lax.ppermute(gram, "gy", pairs)
    chips = count_x * count_y * count_z // 2
    groups = [
        [(x * count_y + y) * count_z + z for x in range(count_x) for y in range(core, count_y, 2) for z in range(count_z)]
        for core in range(2)
    ]
    grams = jnp.broadcast_to(gram[None], (chips, 1, LANES))
    grams = lax.all_to_all(grams, ("gx", "gy", "gz"), 0, 0, tiled=True, axis_index_groups=groups)

    turned = call(
        functools.partial(turn_kernel, count_z),
        jax.ShapeDtypeStruct((count_z, POWERS // 2, extent_x * VARS * extent_z, LANES), F32),
        (pltpu.VMEM((POWERS // 2, extent_x, LANES, LANES), F32),),
    )(basis)
    at_z = lax.axis_index("gz")
    parts = []
    for shift in range(count_z):
        part = lax.dynamic_index_in_dim(turned, (at_z + shift) % count_z, 0, keepdims=False)
        if shift > 0:
            part = lax.ppermute(part, "gz", [(i, (i + shift) % count_z) for i in range(count_z)])
        parts.append(part)
    shape = jax.ShapeDtypeStruct(right_side.shape, F32)
    scratch = pltpu.VMEM((count_z, extent_x * VARS * extent_z, LANES), F32)
    return call(finish_kernel, (shape, shape), (scratch, scratch))(grams, right_side, *parts)


def solution(mesh):
    in_specs = (P(None, "gx", "gz", "gy"), P("gx", "gz", "gy"), P())
    out_specs = (P(None, "gx", "gz", "gy"), P(None, "gx", "gz", "gy"))
    return jax.shard_map(
        per_device, mesh=mesh, in_specs=in_specs, out_specs=out_specs, check_vma=False
    )
```

profile of v0, /device:TPU:1, one launch (start us, length us, event | category | flops | bytes accessed | tf_op | source)
XLA Modules:
  0.0 68.1 jit_solution(13009653222543103160)
XLA Ops:
  0.6 0.0 copy-start.1
  0.6 1.0 %pad_maximum_fusion.fields_ref = f32[6,8,4,256]{3,2,1,0:T(4,128)S(1)} fusion(f32[1,8,4,256]{3,2,1,0:T(4,128)} %bitcast.16, f32[5,8,4,256]{3,2,1,0:T(4,128)} %first_ref.1), kind=kLoop, calls=%fused_computation.4 | loop fusion | flops 49152 | bytes 393216 | tf_op jit(solution)/shard_map/concatenate | solution.py:395
  1.6 0.2 shard_map.50
  1.9 2.6 %collective-permute-start = (f32[2,8,128]{2,1,0:T(8,128)S(1)}, f32[2,8,128]{2,1,0:T(8,128)S(1)}, u32[]{:S(2)}, u32[]{:S(2)}) collective-permute-start(f32[2,8,128]{2,1,0:T(8,128)S(1)} %get-tuple-element.10), channel_id=1, source_target_pairs={{0,4},{4,8},{8,12},{12,16},{16,20},{20,24},{24,28},{28,0},{1,5},{5... | collective-permute-start | bytes 24584 | tf_op jit(solution)/shard_map/ppermute | solution.py:397
  4.5 0.7 collective-permute-start.1
  5.1 0.6 collective-permute-done.left_ref
  5.8 1.8 %collective-permute-done.1.right_ref = f32[2,8,128]{2,1,0:T(8,128)S(1)} collective-permute-done((f32[2,8,128]{2,1,0:T(8,128)S(1)}, f32[2,8,128]{2,1,0:T(8,128)S(1)}, u32[]{:S(2)}, u32[]{:S(2)}) %collective-permute-start.1) | collective-permute-done | bytes 8224 | tf_op jit(solution)/shard_map/ppermute | solution.py:398
  7.6 10.1 %all_to_all.10.here_ref = f32[4,120,128]{2,1,0:T(8,128)S(1)} all-to-all(f32[4,120,128]{2,1,0:T(8,128)S(1)} %shard_map.51), channel_id=1, replica_groups=mesh['gx'=8,'gy'=8,'gz'=4] {'gz'}, dimensions={0} | all-to-all | bytes 491520 | tf_op jit(solution)/shard_map/all_to_all | solution.py:402
  17.7 5.6 %collective-permute-start.3 = (f32[4,120,128]{2,1,0:T(8,128)S(1)}, f32[4,120,128]{2,1,0:T(8,128)S(1)}, u32[]{:S(2)}, u32[]{:S(2)}) collective-permute-start(f32[4,120,128]{2,1,0:T(8,128)S(1)} %all_to_all.10.here_ref), channel_id=1, source_target_pairs={{32,0},{64,32},{96,64},{128,96},{160,128},{192,160},{224,192},{0,2... | collective-permute-start | bytes 737288 | tf_op jit(solution)/shard_map/ppermute | solution.py:405
  23.3 0.0 collective-permute-start.2
  23.3 0.0 copy-done.1
  23.3 0.1 copy.5
  23.4 0.1 reshape.13
  23.5 0.1 copy.6
  23.7 0.2 shard_map.52
  23.9 3.3 %collective-permute-done.3.after_ref = f32[4,120,128]{2,1,0:T(8,128)S(1)} collective-permute-done((f32[4,120,128]{2,1,0:T(8,128)S(1)}, f32[4,120,128]{2,1,0:T(8,128)S(1)}, u32[]{:S(2)}, u32[]{:S(2)}) %collective-permute-start.3) | collective-permute-done | bytes 245792 | tf_op jit(solution)/shard_map/ppermute | solution.py:405
  27.3 3.1 %collective-permute-done.2.before_ref = f32[4,120,128]{2,1,0:T(8,128)S(1)} collective-permute-done((f32[4,120,128]{2,1,0:T(8,128)S(1)}, f32[4,120,128]{2,1,0:T(8,128)S(1)}, u32[]{:S(2)}, u32[]{:S(2)}) %collective-permute-start.2) | collective-permute-done | bytes 245792 | tf_op jit(solution)/shard_map/ppermute | solution.py:404
  30.4 9.3 %shard_map.53 = (f32[9,8,64,128]{3,2,1,0:T(8,128)S(1)}, f32[1,128]{1,0:T(1,128)S(1)}) custom-call(f32[4,120,128]{2,1,0:T(8,128)S(1)} %collective-permute-done.2.before_ref, f32[4,120,128]{2,1,0:T(8,128)S(1)} %all_to_all.10.here_ref, f32[4,120,128]{2,1,0:T(8,128)S(1)} %collective-permute-done.3.after_ref, bf16[384,256]{1,0:T(8,128)(2,1)S(1)} %get-tuple-element.12.spread, ...), custom_call_target="tpu_custom_call" | custom-call | tf_op jit(solution)/shard_map/pallas_call | solution.py:416
  39.7 0.8 %shard_map.54 = f32[4,4,160,128]{3,2,1,0:T(8,128)S(1)} custom-call(f32[9,8,64,128]{3,2,1,0:T(8,128)S(1)} %get-tuple-element.15.basis_ref), custom_call_target="tpu_custom_call" | custom-call | tf_op jit(solution)/shard_map/pallas_call | solution.py:439
  40.5 0.0 copy-start
  40.5 2.6 %collective-permute-start.4 = (f32[1,128]{1,0:T(1,128)S(1)}, f32[1,128]{1,0:T(1,128)S(1)}, u32[]{:S(2)}, u32[]{:S(2)}) collective-permute-start(f32[1,128]{1,0:T(1,128)S(1)} %get-tuple-element.14), channel_id=1, source_target_pairs={{0,4},{4,0},{8,12},{12,8},{16,20},{20,16},{24,28},{28,24},{1,5},{5... | collective-permute-start | bytes 1544 | tf_op jit(solution)/shard_map/ppermute | solution.py:430
  43.1 0.1 dynamic-slice_bitcast_fusion
  43.2 1.1 %collective-permute-start.7 = (f32[4,160,128]{2,1,0:T(8,128)S(1)}, f32[4,160,128]{2,1,0:T(8,128)S(1)}, u32[]{:S(2)}, u32[]{:S(2)}) collective-permute-start(f32[4,160,128]{2,1,0:T(8,128)S(1)} %get-tuple-element.16), channel_id=1, source_target_pairs={{0,3},{1,0},{2,1},{3,2},{4,7},{5,4},{6,5},{7,6},{8,11},{9,8},{10,9... | collective-permute-start | bytes 983048 | tf_op jit(solution)/shard_map/ppermute | solution.py:449
  44.3 1.2 %collective-permute-start.6 = (f32[4,160,128]{2,1,0:T(8,128)S(1)}, f32[4,160,128]{2,1,0:T(8,128)S(1)}, u32[]{:S(2)}, u32[]{:S(2)}) collective-permute-start(f32[4,160,128]{2,1,0:T(8,128)S(1)} %get-tuple-element.17), channel_id=1, source_target_pairs={{0,2},{1,3},{2,0},{3,1},{4,6},{5,7},{6,4},{7,5},{8,10},{9,11},{10,... | collective-permute-start | bytes 983048 | tf_op jit(solution)/shard_map/ppermute | solution.py:449
  45.5 0.0 collective-permute-start.5
  45.5 0.0 collective-permute-done.4
  45.5 21.1 %all_to_all.11.grams_ref = f32[128,1,128]{2,1,0:T(1,128)S(1)} all-to-all(f32[128,1,128]{2,1,0:T(1,128)S(1)} %broadcast_in_dim.17), channel_id=1, replica_groups={{0,1,2,3,8,9,10,11,16,17,18,19,24,25,26,27,32,33,34,35,40,41,42,43,48,4..., dimensions={0} | all-to-all | bytes 131072 | tf_op jit(solution)/shard_map/all_to_all | solution.py:437
  66.6 0.0 collective-permute-done.7.refs_3_
  66.6 0.0 collective-permute-done.6.refs_2_
  66.6 0.0 collective-permute-done.5.refs_1_
  66.6 0.0 copy-done
  66.6 1.5 %shard_map.55 = (f32[5,8,4,256]{3,2,1,0:T(4,128)}, f32[5,8,4,256]{3,2,1,0:T(4,128)}) custom-call(f32[128,1,128]{2,1,0:T(1,128)S(1)} %all_to_all.11.grams_ref, f32[5,8,4,256]{3,2,1,0:T(4,128)S(1)} %copy-done, f32[4,160,128]{2,1,0:T(8,128)S(1)} %get-tuple-element.19.refs_0_, f32[4,160,128]{2,1,0:T(8,128)S(1)} %collective-permute-done.5.refs_1_, ...), custom_call_target="tpu_custom_call" | custom-call | tf_op jit(solution)/shard_map/pallas_call | solution.py:453
  (5 shorter events, 0.1 us)
Async XLA Ops:
  0.6 22.7 %copy-start.1 = (f32[27,5,5]{0,2,1:T(8,128)S(1)}, f32[27,5,5]{0,2,1:T(8,128)}, u32[]{:S(2)}) copy-start(f32[27,5,5]{0,2,1:T(8,128)} %param.5) | copy-start | bytes 8104
  1.9 3.9 %collective-permute-start = (f32[2,8,128]{2,1,0:T(8,128)S(1)}, f32[2,8,128]{2,1,0:T(8,128)S(1)}, u32[]{:S(2)}, u32[]{:S(2)}) collective-permute-start(f32[2,8,128]{2,1,0:T(8,128)S(1)} %get-tuple-element.10), channel_id=1, source_target_pairs={{0,4},{4,8},{8,12},{12,16},{16,20},{20,24},{24,28},{28,0},{1,5},{5... | collective-permute-start | bytes 24584 | tf_op jit(solution)/shard_map/ppermute | solution.py:397
  4.5 3.1 %collective-permute-start.1 = (f32[2,8,128]{2,1,0:T(8,128)S(1)}, f32[2,8,128]{2,1,0:T(8,128)S(1)}, u32[]{:S(2)}, u32[]{:S(2)}) collective-permute-start(f32[2,8,128]{2,1,0:T(8,128)S(1)} %get-tuple-element.11), channel_id=1, source_target_pairs={{4,0},{8,4},{12,8},{16,12},{20,16},{24,20},{28,24},{0,28},{5,1},{9... | collective-permute-start | bytes 24584 | tf_op jit(solution)/shard_map/ppermute | solution.py:398
  17.7 9.5 %collective-permute-start.3 = (f32[4,120,128]{2,1,0:T(8,128)S(1)}, f32[4,120,128]{2,1,0:T(8,128)S(1)}, u32[]{:S(2)}, u32[]{:S(2)}) collective-permute-start(f32[4,120,128]{2,1,0:T(8,128)S(1)} %all_to_all.10.here_ref), channel_id=1, source_target_pairs={{32,0},{64,32},{96,64},{128,96},{160,128},{192,160},{224,192},{0,2... | collective-permute-start | bytes 737288 | tf_op jit(solution)/shard_map/ppermute | solution.py:405
  23.3 7.1 %collective-permute-start.2 = (f32[4,120,128]{2,1,0:T(8,128)S(1)}, f32[4,120,128]{2,1,0:T(8,128)S(1)}, u32[]{:S(2)}, u32[]{:S(2)}) collective-permute-start(f32[4,120,128]{2,1,0:T(8,128)S(1)} %all_to_all.10.here_ref), channel_id=1, source_target_pairs={{0,32},{32,64},{64,96},{96,128},{128,160},{160,192},{192,224},{224... | collective-permute-start | bytes 737288 | tf_op jit(solution)/shard_map/ppermute | solution.py:404
  40.5 26.1 %copy-start = (f32[5,8,4,256]{3,2,1,0:T(4,128)S(1)}, f32[5,8,4,256]{3,2,1,0:T(4,128)}, u32[]{:S(2)}) copy-start(f32[5,8,4,256]{3,2,1,0:T(4,128)} %first_ref.1) | copy-start | bytes 491524
  40.5 5.0 %collective-permute-start.4 = (f32[1,128]{1,0:T(1,128)S(1)}, f32[1,128]{1,0:T(1,128)S(1)}, u32[]{:S(2)}, u32[]{:S(2)}) collective-permute-start(f32[1,128]{1,0:T(1,128)S(1)} %get-tuple-element.14), channel_id=1, source_target_pairs={{0,4},{4,0},{8,12},{12,8},{16,20},{20,16},{24,28},{28,24},{1,5},{5... | collective-permute-start | bytes 1544 | tf_op jit(solution)/shard_map/ppermute | solution.py:430
  43.2 23.5 %collective-permute-start.7 = (f32[4,160,128]{2,1,0:T(8,128)S(1)}, f32[4,160,128]{2,1,0:T(8,128)S(1)}, u32[]{:S(2)}, u32[]{:S(2)}) collective-permute-start(f32[4,160,128]{2,1,0:T(8,128)S(1)} %get-tuple-element.16), channel_id=1, source_target_pairs={{0,3},{1,0},{2,1},{3,2},{4,7},{5,4},{6,5},{7,6},{8,11},{9,8},{10,9... | collective-permute-start | bytes 983048 | tf_op jit(solution)/shard_map/ppermute | solution.py:449
  44.3 22.3 %collective-permute-start.6 = (f32[4,160,128]{2,1,0:T(8,128)S(1)}, f32[4,160,128]{2,1,0:T(8,128)S(1)}, u32[]{:S(2)}, u32[]{:S(2)}) collective-permute-start(f32[4,160,128]{2,1,0:T(8,128)S(1)} %get-tuple-element.17), channel_id=1, source_target_pairs={{0,2},{1,3},{2,0},{3,1},{4,6},{5,7},{6,4},{7,5},{8,10},{9,11},{10,... | collective-permute-start | bytes 983048 | tf_op jit(solution)/shard_map/ppermute | solution.py:449
  45.5 21.1 %collective-permute-start.5 = (f32[4,160,128]{2,1,0:T(8,128)S(1)}, f32[4,160,128]{2,1,0:T(8,128)S(1)}, u32[]{:S(2)}, u32[]{:S(2)}) collective-permute-start(f32[4,160,128]{2,1,0:T(8,128)S(1)} %get-tuple-element.18), channel_id=1, source_target_pairs={{0,1},{1,2},{2,3},{3,0},{4,5},{5,6},{6,7},{7,4},{8,9},{9,10},{10,1... | collective-permute-start | bytes 983048 | tf_op jit(solution)/shard_map/ppermute | solution.py:449
where the time goes:
time: 68.3 us; the launch traced here: 68.1 us
  blocking collectives  31.2 us (46%)
  starting transfers between devices  13.8 us (20%)
  Pallas kernels  12 us (18%)
  waiting for transfers between devices  8.89 us (13%)
  other arithmetic  0.99 us (1%)
  between operations  0.77 us (1%)
    all_to_all x1, blocking collectives, per_device(): lax.all_to_all(grams, ('gx', 'gy', 'gz'), 0, 0, tiled=True, axis_index_gr...  21.1 us
    all_to_all x1, blocking collectives, per_device(): here = lax.all_to_all(strips, 'gz', 0, 0, tiled=True)  10.1 us
    pallas_call x1, Pallas kernels, per_device(): call(functools.partial(powers_kernel, extent_x, extent_z), (jax.ShapeDtyp...  9.29 us
    ppermute x1, starting transfers between devices, per_device(): after = lax.ppermute(here, 'gx', down)  5.58 us
    ppermute x1, waiting for transfers between devices, per_device(): after = lax.ppermute(here, 'gx', down)  3.34 us
    ppermute x1, waiting for transfers between devices, per_device(): before = lax.ppermute(here, 'gx', up)  3.13 us
    ppermute x1, starting transfers between devices, per_device(): left = lax.ppermute(last, 'gy', up)  2.61 us
    ppermute x1, starting transfers between devices, per_device(): gram = gram + lax.ppermute(gram, 'gy', pairs)  2.57 us
  transfers between devices with their start and end apart: 8, of which 4 were waited for; matrix products, arithmetic and copies ran while one was open for 1% of the time, Pallas kernels for 0%

commit v1 on v0

--- a/solution.py
+++ b/solution.py
@@ -129,92 +129,153 @@
     matrix[4 * LANES :, :] = low
 
 
-def powers_kernel(
-    own_x, extent_z, before_ref, here_ref, after_ref, spread, matrix, basis_ref, gram_ref, even, odd, cond
-):
-    peers = here_ref.shape[0]
-    wide_y = cond.shape[1]
-    size_z = peers * extent_z
-    used = VARS * size_z
+def planes_of(ref, spread, own_x, extent_z, wide_y):
+    peers = ref.shape[0]
     group = FIELDS * extent_z
     half = own_x // 2
+    lane = lane_iota(wide_y)
+    whole, rest = [], []
+    for peer in range(peers):
+        whole.append(ref[peer, :wide_y])
+        packed = ref[peer, wide_y:]
+        rest.append(jnp.concatenate([packed, roll_lanes(packed, LANES // 2)], axis=0))
+
+    def moved(peer, start):
+        place = peer * group
+        if start >= LANES:
+            return roll_lanes(rest[peer], place - (start - LANES))
+        value = roll_lanes(whole[peer], place - start)
+        if start + group > LANES:
+            edge = place + LANES - start
+            value = jnp.where(lane < edge, value, roll_lanes(rest[peer], edge))
+        return value
+
+    planes = []
+    for part in range(2):
+        gathered = []
+        for x_local in range(half):
+            start = (part * half + x_local) * group
+            total = moved(0, start)
+            for peer in range(1, peers):
+                total = jnp.where(lane < peer * group, total, moved(peer, start))
+            gathered.append(total)
+        split = pieces_of(jnp.concatenate(gathered, axis=0), 3)
+        result = jnp.dot(jnp.concatenate(split, axis=1), spread[...], preferred_element_type=F32)
+        for x_local in range(half):
+            rows = slice(x_local * wide_y, (x_local + 1) * wide_y)
+            planes.append((result[rows, :LANES], result[rows, LANES:]))
+    return planes
+
+
+def within(block, peers, own_y, wide_y):
+    at_x, at_y, at_z = (lax.axis_index(axis) for axis in ("gx", "gy", "gz"))
+    column = row_iota(wide_y) + ((at_y * peers + at_z) * own_y - HALO)
+    inside = (column >= 0) & (column < lax.axis_size("gy") * peers * own_y)
+    block_x = at_x + (block - 1)
+    return inside & (block_x >= 0) & (block_x < lax.axis_size("gx"))
+
+
+def apply(used, wide_y, matrix, x_from, x_to, get, weight_of, put):
+    lane = lane_iota(wide_y)
+    near = [get(x_at) for x_at in range(x_from - 1, x_to + 1)]
+    firsts, seconds = [], []
+    for at in range(x_to - x_from):
+        middle = roll_lanes(near[at + 1], used)
+        firsts.append(jnp.where(lane < used, near[at], middle))
+        last = roll_lanes(near[at + 2], 2 * used)
+        seconds.append(jnp.where(lane < 2 * used - LANES, middle, last))
+    stacked = jnp.concatenate([jnp.concatenate(firsts, axis=0), jnp.concatenate(seconds, axis=0)], axis=1)
+    high, low = pieces_of(stacked, 2)
+    product = jnp.dot(jnp.concatenate([high, low, high], axis=1), matrix[...], preferred_element_type=F32)
+    for at in range(x_to - x_from):
+        left = product[at * wide_y : (at + 1) * wide_y, :LANES]
+        right = product[at * wide_y : (at + 1) * wide_y, LANES:]
+        ahead = jnp.where(lane < LANES - used, roll_lanes(left, -used), roll_lanes(right, -2 * used))
+        total = left + pltpu.roll(right, 1, 0) + pltpu.roll(ahead, wide_y - 1, 0)
+        weight = weight_of(x_from + at)
+        value = weight * total
+        put(x_from + at, value, weight * value)
+
+
+def own_kernel(own_x, extent_z, here_ref, spread, matrix, cond_ref, scaled_ref, basis_ref):
+    peers = here_ref.shape[0]
+    wide_y, own_y = scaled_ref.shape[2], basis_ref.shape[2]
+    used = VARS * peers * extent_z
+    inside = within(1, peers, own_y, wide_y)
+    for at, (field, weight) in enumerate(planes_of(here_ref, spread, own_x, extent_z, wide_y)):
+        weight = jnp.where(inside, weight, 0.0)
+        cond_ref[at] = weight
+        scaled_ref[0, at] = weight * field
+        basis_ref[0, at] = field[HALO : HALO + own_y]
+    for power in range(1, STEPS):
+
+        def get(x_at, power=power):
+            return scaled_ref[power - 1, x_at]
+
+        def put(x_at, value, scaled, power=power):
+            basis_ref[power, x_at] = value[HALO : HALO + own_y]
+            scaled_ref[power, x_at] = scaled
+
+        apply(used, wide_y, matrix, power, own_x - power, get, lambda x_at: cond_ref[x_at], put)
+
+
+def powers_kernel(
+    own_x,
+    extent_z,
+    before_ref,
+    after_ref,
+    own_cond,
+    own_scaled,
+    own_basis,
+    spread,
+    matrix,
+    basis_ref,
+    gram_ref,
+    even,
+    odd,
+    cond,
+):
+    peers = before_ref.shape[0]
+    _, wide_y, _ = cond.shape
+    used = VARS * peers * extent_z
     wide_x = 3 * own_x
     own_y = wide_y - 2 * HALO
-
-    at_x, at_y, at_z = (lax.axis_index(axis) for axis in ("gx", "gy", "gz"))
-    count_x, count_y = lax.axis_size("gx"), lax.axis_size("gy")
-    column_y = row_iota(wide_y) + ((at_y * peers + at_z) * own_y - HALO)
-    inside_y = (column_y >= 0) & (column_y < count_y * peers * own_y)
-    lane = lane_iota(wide_y)
-    for block, ref in enumerate((before_ref, here_ref, after_ref)):
-        block_x = at_x + (block - 1)
-        inside = inside_y & (block_x >= 0) & (block_x < count_x)
-        whole, rest = [], []
-        for peer in range(peers):
-            whole.append(ref[peer, :wide_y])
-            packed = ref[peer, wide_y:]
-            rest.append(jnp.concatenate([packed, roll_lanes(packed, LANES // 2)], axis=0))
-
-        def moved(peer, start):
-            place = peer * group
-            if start >= LANES:
-                return roll_lanes(rest[peer], place - (start - LANES))
-            value = roll_lanes(whole[peer], place - start)
-            if start + group > LANES:
-                edge = place + LANES - start
-                value = jnp.where(lane < edge, value, roll_lanes(rest[peer], edge))
-            return value
-
-        for part in range(2):
-            gathered = []
-            for x_local in range(half):
-                start = (part * half + x_local) * group
-                total = moved(0, start)
-                for peer in range(1, peers):
-                    total = jnp.where(lane < peer * group, total, moved(peer, start))
-                gathered.append(total)
-            split = pieces_of(jnp.concatenate(gathered, axis=0), 3)
-            result = jnp.dot(jnp.concatenate(split, axis=1), spread[...], preferred_element_type=F32)
-            for x_local in range(half):
-                x_at = (block * 2 + part) * half + x_local
-                rows = slice(x_local * wide_y, (x_local + 1) * wide_y)
-                field = result[rows, :LANES]
-                weight = jnp.where(inside, result[rows, LANES:], 0.0)
-                cond[x_at] = weight
-                even[x_at + 1] = weight * field
-                if block == 1:
-                    basis_ref[0, part * half + x_local] = field[HALO : HALO + own_y]
-
-    def apply(power, now, later, x_from, count):
-        near = [now[x_from + at] for at in range(count + 2)]
-        firsts, seconds = [], []
-        for at in range(count):
-            middle = roll_lanes(near[at + 1], used)
-            firsts.append(jnp.where(lane < used, near[at], middle))
-            last = roll_lanes(near[at + 2], 2 * used)
-            seconds.append(jnp.where(lane < 2 * used - LANES, middle, last))
-        stacked = jnp.concatenate(
-            [jnp.concatenate(firsts, axis=0), jnp.concatenate(seconds, axis=0)], axis=1
-        )
-        high, low = pieces_of(stacked, 2)
-        product = jnp.dot(jnp.concatenate([high, low, high], axis=1), matrix[...], preferred_element_type=F32)
-        for at in range(count):
-            x_at = x_from + at
-            left = product[at * wide_y : (at + 1) * wide_y, :LANES]
-            right = product[at * wide_y : (at + 1) * wide_y, LANES:]
-            ahead = jnp.where(lane < LANES - used, roll_lanes(left, -used), roll_lanes(right, -2 * used))
-            total = left + pltpu.roll(right, 1, 0) + pltpu.roll(ahead, wide_y - 1, 0)
-            weight = cond[x_at]
-            value = weight * total
-            if 0 <= x_at - own_x < own_x:
+    slots = (even, odd)
+
+    def known(power, x_at):
+        return power < STEPS and own_x + power <= x_at < 2 * own_x - power
+
+    for block, ref in ((0, before_ref), (2, after_ref)):
+        inside = within(block, peers, own_y, wide_y)
+        for at, (field, weight) in enumerate(planes_of(ref, spread, own_x, extent_z, wide_y)):
+            weight = jnp.where(inside, weight, 0.0)
+            cond[block * own_x + at] = weight
+            even[block * own_x + at] = weight * field
+    for power in range(STEPS):
+        for at in range(power, own_x - power):
+            basis_ref[power, at] = own_basis[power, at]
+
+    def weight_of(x_at):
+        return own_cond[x_at - own_x] if own_x <= x_at < 2 * own_x else cond[x_at]
+
+    for power in range(1, POWERS + 1):
+
+        def get(x_at, power=power):
+            if known(power - 1, x_at):
+                return own_scaled[power - 1, x_at - own_x]
+            return slots[(power - 1) % 2][x_at]
+
+        def put(x_at, value, scaled, power=power):
+            if own_x <= x_at < 2 * own_x:
                 basis_ref[power, x_at - own_x] = value[HALO : HALO + own_y]
             if power < POWERS:
-                later[x_at + 1] = weight * value
-
-    slots = (even, odd)
-    for power in range(1, POWERS + 1):
-        for x_from, x_to in spans(power, wide_x - power):
-            apply(power, slots[(power + 1) % 2], slots[power % 2], x_from, x_to - x_from)
+                slots[power % 2][x_at] = scaled
+
+        missing = [x_at for x_at in range(power, wide_x - power) if not known(power, x_at)]
+        cuts = [at for at in range(1, len(missing)) if missing[at] != missing[at - 1] + 1]
+        for first, last in zip([0] + cuts, cuts + [len(missing)]):
+            for x_from, x_to in spans(missing[first], missing[last - 1] + 1):
+                apply(used, wide_y, matrix, x_from, x_to, get, weight_of, put)
 
     def add(x_at, sums):
         for tile in range(own_y // 8):
@@ -413,18 +474,23 @@
             jax.ShapeDtypeStruct((6 * LANES, 2 * LANES), BF16),
         ),
     )(rows)
+    own = call(
+        functools.partial(own_kernel, extent_x, extent_z),
+        (
+            jax.ShapeDtypeStruct((extent_x, wide_y, LANES), F32),
+            jax.ShapeDtypeStruct((STEPS, extent_x, wide_y, LANES), F32),
+            jax.ShapeDtypeStruct((STEPS, extent_x, own_y, LANES), F32),
+        ),
+    )(here, spread, matrix)
+    planes = pltpu.VMEM((3 * extent_x, wide_y, LANES), F32)
     basis, gram = call(
         functools.partial(powers_kernel, extent_x, extent_z),
         (
             jax.ShapeDtypeStruct((POWERS + 1, extent_x, own_y, LANES), F32),
             jax.ShapeDtypeStruct((1, LANES), F32),
         ),
-        (
-            pltpu.VMEM((3 * extent_x + 2, wide_y, LANES), F32),
-            pltpu.VMEM((3 * extent_x + 2, wide_y, LANES), F32),
-            pltpu.VMEM((3 * extent_x, wide_y, LANES), F32),
-        ),
-    )(before, here, after, spread, matrix)
+        (planes, planes, planes),
+    )(before, after, *own, spread, matrix)
 
     pairs = [(i, i ^ 1) for i in range(count_y)]
     gram = gram + lax.ppermute(gram, "gy", pairs)

time: 68.3 us -> 67.6 us (0.990)
  waiting for transfers between devices: 8.89 us -> 4.79 us
  blocking collectives: 31.2 us -> 33.5 us
  Pallas kernels: 12 us -> 13.1 us
    ppermute x1, waiting for transfers between devices: 3.34 us -> 0.01 us  [per_device(): after = lax.ppermute(here, 'gx', down)]
    all_to_all x1, blocking collectives: 21.1 us -> 23.3 us  [per_device(): lax.all_to_all(grams, ('gx', 'gy', 'gz'), 0, 0, tiled=True, axis_index_gr...]
    pallas_call x0 -> x1, Pallas kernels: none -> 1.98 us  [per_device(): call(functools.partial(own_kernel, extent_x, extent_z), (jax.ShapeDtypeSt...]
    ppermute x1, starting transfers between devices: 0.01 us -> 1.64 us  [per_device(): before = lax.ppermute(here, 'gx', up)]
    ppermute x1, starting transfers between devices: 5.58 us -> 3.94 us  [per_device(): after = lax.ppermute(here, 'gx', down)]
    pallas_call x1, Pallas kernels: 9.29 us -> 8.46 us  [per_device(): call(functools.partial(powers_kernel, extent_x, extent_z), (jax.ShapeDtyp...]
    ppermute x1, waiting for transfers between devices: 3.13 us -> 2.37 us  [per_device(): before = lax.ppermute(here, 'gx', up)]
  transfers between devices with their start and end apart: 8 -> 8, of which waited for: 4 -> 3; matrix products, arithmetic and copies ran while one was open for 1% -> 1% of each run, Pallas kernels for 0% -> 4%
where the time goes in v1:
time: 67.6 us; the launch traced here: 67.4 us
  blocking collectives  33.5 us (50%)
  starting transfers between devices  13.8 us (20%)
  Pallas kernels  13.1 us (19%)
  waiting for transfers between devices  4.79 us (7%)
  other arithmetic  0.99 us (1%)
  between operations  0.77 us (1%)
    all_to_all x1, blocking collectives, per_device(): lax.all_to_all(grams, ('gx', 'gy', 'gz'), 0, 0, tiled=True, axis_index_gr...  23.3 us
    all_to_all x1, blocking collectives, per_device(): here = lax.all_to_all(strips, 'gz', 0, 0, tiled=True)  10.1 us
    pallas_call x1, Pallas kernels, per_device(): call(functools.partial(powers_kernel, extent_x, extent_z), (jax.ShapeDtyp...  8.46 us
    ppermute x1, starting transfers between devices, per_device(): after = lax.ppermute(here, 'gx', down)  3.94 us
    ppermute x3, starting transfers between devices, per_device(): lax.ppermute(part, 'gz', [(i, (i + shift) % count_z) for i in range(count...  2.86 us
    ppermute x1, starting transfers between devices, per_device(): left = lax.ppermute(last, 'gy', up)  2.61 us
    ppermute x1, waiting for transfers between devices, per_device(): before = lax.ppermute(here, 'gx', up)  2.37 us
    ppermute x1, starting transfers between devices, per_device(): gram = gram + lax.ppermute(gram, 'gy', pairs)  2.09 us
  transfers between devices with their start and end apart: 8, of which 3 were waited for; matrix products, arithmetic and copies ran while one was open for 1% of the time, Pallas kernels for 4%

profile of v1, /device:TPU:1, one launch (start us, length us, event | category | flops | bytes accessed | tf_op | source)
XLA Modules:
  0.0 67.4 jit_solution(4616352585663435725)
XLA Ops:
  0.6 0.0 copy-start.1
  0.6 1.0 %pad_maximum_fusion.fields_ref = f32[6,8,4,256]{3,2,1,0:T(4,128)S(1)} fusion(f32[1,8,4,256]{3,2,1,0:T(4,128)} %bitcast.16, f32[5,8,4,256]{3,2,1,0:T(4,128)} %first_ref.1), kind=kLoop, calls=%fused_computation.4 | loop fusion | flops 49152 | bytes 393216 | tf_op jit(solution)/shard_map/concatenate | solution.py:456
  1.6 0.2 shard_map.50
  1.9 2.6 %collective-permute-start = (f32[2,8,128]{2,1,0:T(8,128)S(1)}, f32[2,8,128]{2,1,0:T(8,128)S(1)}, u32[]{:S(2)}, u32[]{:S(2)}) collective-permute-start(f32[2,8,128]{2,1,0:T(8,128)S(1)} %get-tuple-element.13), channel_id=1, source_target_pairs={{0,4},{4,8},{8,12},{12,16},{16,20},{20,24},{24,28},{28,0},{1,5},{5... | collective-permute-start | bytes 24584 | tf_op jit(solution)/shard_map/ppermute | solution.py:458
  4.5 0.7 collective-permute-start.1
  5.1 0.6 collective-permute-done.left_ref
  5.8 1.8 %collective-permute-done.1.right_ref = f32[2,8,128]{2,1,0:T(8,128)S(1)} collective-permute-done((f32[2,8,128]{2,1,0:T(8,128)S(1)}, f32[2,8,128]{2,1,0:T(8,128)S(1)}, u32[]{:S(2)}, u32[]{:S(2)}) %collective-permute-start.1) | collective-permute-done | bytes 8224 | tf_op jit(solution)/shard_map/ppermute | solution.py:459
  7.6 10.1 %all_to_all.10.here_ref = f32[4,120,128]{2,1,0:T(8,128)S(1)} all-to-all(f32[4,120,128]{2,1,0:T(8,128)S(1)} %shard_map.51), channel_id=1, replica_groups=mesh['gx'=8,'gy'=8,'gz'=4] {'gz'}, dimensions={0} | all-to-all | bytes 491520 | tf_op jit(solution)/shard_map/all_to_all | solution.py:463
  17.7 1.6 %collective-permute-start.2 = (f32[4,120,128]{2,1,0:T(8,128)S(1)}, f32[4,120,128]{2,1,0:T(8,128)S(1)}, u32[]{:S(2)}, u32[]{:S(2)}) collective-permute-start(f32[4,120,128]{2,1,0:T(8,128)S(1)} %all_to_all.10.here_ref), channel_id=1, source_target_pairs={{0,32},{32,64},{64,96},{96,128},{128,160},{160,192},{192,224},{224... | collective-permute-start | bytes 737288 | tf_op jit(solution)/shard_map/ppermute | solution.py:465
  19.4 3.9 %collective-permute-start.3 = (f32[4,120,128]{2,1,0:T(8,128)S(1)}, f32[4,120,128]{2,1,0:T(8,128)S(1)}, u32[]{:S(2)}, u32[]{:S(2)}) collective-permute-start(f32[4,120,128]{2,1,0:T(8,128)S(1)} %all_to_all.10.here_ref), channel_id=1, source_target_pairs={{32,0},{64,32},{96,64},{128,96},{160,128},{192,160},{224,192},{0,2... | collective-permute-start | bytes 737288 | tf_op jit(solution)/shard_map/ppermute | solution.py:466
  23.3 0.0 copy-done.1
  23.3 0.1 copy.5
  23.4 0.1 reshape.13
  23.5 0.1 copy.6
  23.7 0.2 shard_map.52
  23.9 2.0 %shard_map.53 = (f32[8,80,128]{2,1,0:T(8,128)S(1)}, f32[4,8,80,128]{3,2,1,0:T(8,128)S(1)}, f32[4,8,64,128]{3,2,1,0:T(8,128)S(1)}) custom-call(f32[4,120,128]{2,1,0:T(8,128)S(1)} %all_to_all.10.here_ref, bf16[384,256]{1,0:T(8,128)(2,1)S(1)} %get-tuple-element.15.spread, bf16[768,256]{1,0:T(8,128)(2,1)S(1)} %get-tuple-element.16.matrix), custom_call_target="tpu_custom_call" | custom-call | tf_op jit(solution)/shard_map/pallas_call | solution.py:477
  25.9 2.4 %collective-permute-done.2.before_ref = f32[4,120,128]{2,1,0:T(8,128)S(1)} collective-permute-done((f32[4,120,128]{2,1,0:T(8,128)S(1)}, f32[4,120,128]{2,1,0:T(8,128)S(1)}, u32[]{:S(2)}, u32[]{:S(2)}) %collective-permute-start.2) | collective-permute-done | bytes 245792 | tf_op jit(solution)/shard_map/ppermute | solution.py:465
  28.3 0.0 collective-permute-done.3.after_ref
  28.3 8.5 %shard_map.54 = (f32[9,8,64,128]{3,2,1,0:T(8,128)S(1)}, f32[1,128]{1,0:T(1,128)S(1)}) custom-call(f32[4,120,128]{2,1,0:T(8,128)S(1)} %collective-permute-done.2.before_ref, f32[4,120,128]{2,1,0:T(8,128)S(1)} %collective-permute-done.3.after_ref, f32[8,80,128]{2,1,0:T(8,128)S(1)} %get-tuple-element.17.own_cond, ...), custom_call_target="tpu_custom_call" | custom-call | tf_op jit(solution)/shard_map/pallas_call | solution.py:486
  36.7 2.1 %collective-permute-start.4 = (f32[1,128]{1,0:T(1,128)S(1)}, f32[1,128]{1,0:T(1,128)S(1)}, u32[]{:S(2)}, u32[]{:S(2)}) collective-permute-start(f32[1,128]{1,0:T(1,128)S(1)} %get-tuple-element.20), channel_id=1, source_target_pairs={{0,4},{4,0},{8,12},{12,8},{16,20},{20,16},{24,28},{28,24},{1,5},{5... | collective-permute-start | bytes 1544 | tf_op jit(solution)/shard_map/ppermute | solution.py:496
  38.8 0.8 %shard_map.55 = f32[4,4,160,128]{3,2,1,0:T(8,128)S(1)} custom-call(f32[9,8,64,128]{3,2,1,0:T(8,128)S(1)} %get-tuple-element.21.basis_ref), custom_call_target="tpu_custom_call" | custom-call | tf_op jit(solution)/shard_map/pallas_call | solution.py:505
  39.6 0.0 copy-start
  39.6 0.1 dynamic-slice_bitcast_fusion
  39.7 0.4 collective-permute-start.5
  40.1 1.8 %collective-permute-start.6 = (f32[4,160,128]{2,1,0:T(8,128)S(1)}, f32[4,160,128]{2,1,0:T(8,128)S(1)}, u32[]{:S(2)}, u32[]{:S(2)}) collective-permute-start(f32[4,160,128]{2,1,0:T(8,128)S(1)} %get-tuple-element.23), channel_id=1, source_target_pairs={{0,2},{1,3},{2,0},{3,1},{4,6},{5,7},{6,4},{7,5},{8,10},{9,11},{10,... | collective-permute-start | bytes 983048 | tf_op jit(solution)/shard_map/ppermute | solution.py:515
  41.9 0.7 %collective-permute-start.7 = (f32[4,160,128]{2,1,0:T(8,128)S(1)}, f32[4,160,128]{2,1,0:T(8,128)S(1)}, u32[]{:S(2)}, u32[]{:S(2)}) collective-permute-start(f32[4,160,128]{2,1,0:T(8,128)S(1)} %get-tuple-element.22), channel_id=1, source_target_pairs={{0,3},{1,0},{2,1},{3,2},{4,7},{5,4},{6,5},{7,6},{8,11},{9,8},{10,9... | collective-permute-start | bytes 983048 | tf_op jit(solution)/shard_map/ppermute | solution.py:515
  42.6 0.0 collective-permute-done.4
  42.6 23.3 %all_to_all.11.grams_ref = f32[128,1,128]{2,1,0:T(1,128)S(1)} all-to-all(f32[128,1,128]{2,1,0:T(1,128)S(1)} %broadcast_in_dim.17), channel_id=1, replica_groups={{0,1,2,3,8,9,10,11,16,17,18,19,24,25,26,27,32,33,34,35,40,41,42,43,48,4..., dimensions={0} | all-to-all | bytes 131072 | tf_op jit(solution)/shard_map/all_to_all | solution.py:503
  65.9 0.0 collective-permute-done.5.refs_1_
  65.9 0.0 collective-permute-done.6.refs_2_
  65.9 0.0 collective-permute-done.7.refs_3_
  66.0 1.5 %shard_map.56 = (f32[5,8,4,256]{3,2,1,0:T(4,128)}, f32[5,8,4,256]{3,2,1,0:T(4,128)}) custom-call(f32[128,1,128]{2,1,0:T(1,128)S(1)} %all_to_all.11.grams_ref, f32[5,8,4,256]{3,2,1,0:T(4,128)S(1)} %copy-done, f32[4,160,128]{2,1,0:T(8,128)S(1)} %get-tuple-element.25.refs_0_, f32[4,160,128]{2,1,0:T(8,128)S(1)} %collective-permute-done.5.refs_1_, ...), custom_call_target="tpu_custom_call" | custom-call | tf_op jit(solution)/shard_map/pallas_call | solution.py:519
  (6 shorter events, 0.1 us)
Async XLA Ops:
  0.6 22.7 %copy-start.1 = (f32[27,5,5]{0,2,1:T(8,128)S(1)}, f32[27,5,5]{0,2,1:T(8,128)}, u32[]{:S(2)}) copy-start(f32[27,5,5]{0,2,1:T(8,128)} %param.5) | copy-start | bytes 8104
  1.9 3.9 %collective-permute-start = (f32[2,8,128]{2,1,0:T(8,128)S(1)}, f32[2,8,128]{2,1,0:T(8,128)S(1)}, u32[]{:S(2)}, u32[]{:S(2)}) collective-permute-start(f32[2,8,128]{2,1,0:T(8,128)S(1)} %get-tuple-element.13), channel_id=1, source_target_pairs={{0,4},{4,8},{8,12},{12,16},{16,20},{20,24},{24,28},{28,0},{1,5},{5... | collective-permute-start | bytes 24584 | tf_op jit(solution)/shard_map/ppermute | solution.py:458
  4.5 3.1 %collective-permute-start.1 = (f32[2,8,128]{2,1,0:T(8,128)S(1)}, f32[2,8,128]{2,1,0:T(8,128)S(1)}, u32[]{:S(2)}, u32[]{:S(2)}) collective-permute-start(f32[2,8,128]{2,1,0:T(8,128)S(1)} %get-tuple-element.14), channel_id=1, source_target_pairs={{4,0},{8,4},{12,8},{16,12},{20,16},{24,20},{28,24},{0,28},{5,1},{9... | collective-permute-start | bytes 24584 | tf_op jit(solution)/shard_map/ppermute | solution.py:459
  17.7 10.6 %collective-permute-start.2 = (f32[4,120,128]{2,1,0:T(8,128)S(1)}, f32[4,120,128]{2,1,0:T(8,128)S(1)}, u32[]{:S(2)}, u32[]{:S(2)}) collective-permute-start(f32[4,120,128]{2,1,0:T(8,128)S(1)} %all_to_all.10.here_ref), channel_id=1, source_target_pairs={{0,32},{32,64},{64,96},{96,128},{128,160},{160,192},{192,224},{224... | collective-permute-start | bytes 737288 | tf_op jit(solution)/shard_map/ppermute | solution.py:465
  19.4 8.9 %collective-permute-start.3 = (f32[4,120,128]{2,1,0:T(8,128)S(1)}, f32[4,120,128]{2,1,0:T(8,128)S(1)}, u32[]{:S(2)}, u32[]{:S(2)}) collective-permute-start(f32[4,120,128]{2,1,0:T(8,128)S(1)} %all_to_all.10.here_ref), channel_id=1, source_target_pairs={{32,0},{64,32},{96,64},{128,96},{160,128},{192,160},{224,192},{0,2... | collective-permute-start | bytes 737288 | tf_op jit(solution)/shard_map/ppermute | solution.py:466
  36.7 5.8 %collective-permute-start.4 = (f32[1,128]{1,0:T(1,128)S(1)}, f32[1,128]{1,0:T(1,128)S(1)}, u32[]{:S(2)}, u32[]{:S(2)}) collective-permute-start(f32[1,128]{1,0:T(1,128)S(1)} %get-tuple-element.20), channel_id=1, source_target_pairs={{0,4},{4,0},{8,12},{12,8},{16,20},{20,16},{24,28},{28,24},{1,5},{5... | collective-permute-start | bytes 1544 | tf_op jit(solution)/shard_map/ppermute | solution.py:496
  39.6 26.4 %copy-start = (f32[5,8,4,256]{3,2,1,0:T(4,128)S(1)}, f32[5,8,4,256]{3,2,1,0:T(4,128)}, u32[]{:S(2)}) copy-start(f32[5,8,4,256]{3,2,1,0:T(4,128)} %first_ref.1) | copy-start | bytes 491524
  39.7 26.2 %collective-permute-start.5 = (f32[4,160,128]{2,1,0:T(8,128)S(1)}, f32[4,160,128]{2,1,0:T(8,128)S(1)}, u32[]{:S(2)}, u32[]{:S(2)}) collective-permute-start(f32[4,160,128]{2,1,0:T(8,128)S(1)} %get-tuple-element.24), channel_id=1, source_target_pairs={{0,1},{1,2},{2,3},{3,0},{4,5},{5,6},{6,7},{7,4},{8,9},{9,10},{10,1... | collective-permute-start | bytes 983048 | tf_op jit(solution)/shard_map/ppermute | solution.py:515
  40.1 25.9 %collective-permute-start.6 = (f32[4,160,128]{2,1,0:T(8,128)S(1)}, f32[4,160,128]{2,1,0:T(8,128)S(1)}, u32[]{:S(2)}, u32[]{:S(2)}) collective-permute-start(f32[4,160,128]{2,1,0:T(8,128)S(1)} %get-tuple-element.23), channel_id=1, source_target_pairs={{0,2},{1,3},{2,0},{3,1},{4,6},{5,7},{6,4},{7,5},{8,10},{9,11},{10,... | collective-permute-start | bytes 983048 | tf_op jit(solution)/shard_map/ppermute | solution.py:515
  41.9 24.1 %collective-permute-start.7 = (f32[4,160,128]{2,1,0:T(8,128)S(1)}, f32[4,160,128]{2,1,0:T(8,128)S(1)}, u32[]{:S(2)}, u32[]{:S(2)}) collective-permute-start(f32[4,160,128]{2,1,0:T(8,128)S(1)} %get-tuple-element.22), channel_id=1, source_target_pairs={{0,3},{1,0},{2,1},{3,2},{4,7},{5,4},{6,5},{7,6},{8,11},{9,8},{10,9... | collective-permute-start | bytes 983048 | tf_op jit(solution)/shard_map/ppermute | solution.py:515
